TPU v7x, 32 devices: a whole 2x2x4 slice. The times are simulated.
32 devices in a mesh: dp: 4 (over x, core), fsdp: 8 (over z, y).
Axes of the slice: x: 2, y: 2, z: 4, core: 2. Of those that a mesh axis runs over, the one named last changes fastest.
Arguments:
- hidden_input: bfloat16 [4, 2, 1024, 8192], P('dp', None, 'fsdp'), may hold values from -6 to 6
- readout: bfloat16 [4, 2, 1024, 512], P('dp', None, 'fsdp'), may hold values from -0.26367188 to 0.26367188
- response: int32 [4, 2, 1024], P('dp', None, 'fsdp'), may hold values from 0 to 1, as said below
- value_matrix: bfloat16 [8192, 512], P('fsdp'), may hold values from -0.0625 to 0.0625
- adapter_down: bfloat16 [8192, 64], P('fsdp'), may hold values from -0.0625 to 0.0625
- adapter_up: bfloat16 [64, 512], replicated, may hold values from -0.037353516 to 0.037353516
Outputs:
- down_gradient: float32 [8192, 64], P('fsdp')
- grad_b_t: float32 [512, 64], P('fsdp')
- losses: float32 [4], P('dp')
- margins: float32 [4], P('dp')
Inputs may be any that keep to these rules, and one draw needn't show every extreme that they name: `response`: each sequence's 1s form one contiguous run of tokens that starts between 128 and 512 and ends between 768 and 1024.
All inputs are finite; a program needn't handle non-finite values.
Results may differ from a plain program's by a relative error of at most 0.0055.
Values may be sent and summed in bfloat16 or wider, within the bound.
A program may use at most 64 MiB of HBM per device.

v0:
```python
import jax
import jax.numpy as jnp
from jax import lax
from jax.sharding import PartitionSpec as P

DPO_BETA = 0.5
ADAPTER_SCALE = 2.0


def shards(hidden_input, readout, response, value_matrix, adapter_down, adapter_up):
    seq_rows = hidden_input.shape[2]
    width = hidden_input.shape[3]
    kv_width = value_matrix.shape[1]
    token_row_block = hidden_input.reshape(2 * seq_rows, width)
    base_output = jnp.dot(
        token_row_block,
        lax.all_gather(value_matrix, "fsdp", axis=0, tiled=True),
        preferred_element_type=jnp.float32,
    )
    low_sum = jnp.dot(
        token_row_block,
        lax.all_gather(adapter_down, "fsdp", axis=0, tiled=True),
        preferred_element_type=jnp.float32,
    )
    lowrank_output = low_sum.astype(jnp.bfloat16)
    policy_score = base_output + ADAPTER_SCALE * jnp.dot(
        lowrank_output, adapter_up, preferred_element_type=jnp.float32
    )
    read_f = readout.reshape(2 * seq_rows, kv_width).astype(jnp.float32)
    mask_f = response.reshape(2 * seq_rows).astype(jnp.float32)
    t_pol = jnp.tanh(policy_score)
    t_ref = jnp.tanh(base_output)
    scores = jnp.sum(read_f * (t_pol - t_ref), axis=1) * mask_f
    partial_value = jnp.sum(scores.reshape(2, seq_rows), axis=1)
    ratio = lax.psum(partial_value, "fsdp")
    reward_margin = DPO_BETA * (ratio[0] - ratio[1])
    pair_loss_total = jax.nn.softplus(-reward_margin)
    gate = jax.nn.sigmoid(-reward_margin)
    coef = DPO_BETA * gate * jnp.array([-1.0, 1.0], jnp.float32)
    coef_rows = jnp.repeat(coef, seq_rows)
    hidden_gradient = (
        coef_rows[:, None] * mask_f[:, None] * read_f * (1.0 - t_pol * t_pol)
    ).astype(jnp.bfloat16)
    up_gradient_flipped = ADAPTER_SCALE * lax.dot_general(
        hidden_gradient,
        lowrank_output,
        (((0,), (0,)), ((), ())),
        preferred_element_type=jnp.float32,
    )
    lowrank_gradient = (
        ADAPTER_SCALE
        * lax.dot_general(
            hidden_gradient,
            adapter_up,
            (((1,), (1,)), ((), ())),
            preferred_element_type=jnp.float32,
        )
    ).astype(jnp.bfloat16)
    down_gradient = lax.dot_general(
        token_row_block,
        lowrank_gradient,
        (((0,), (0,)), ((), ())),
        preferred_element_type=jnp.float32,
    )
    summed_a, summed_b = lax.psum((down_gradient, up_gradient_flipped), "dp")
    part_a, part_b = (
        lax.psum_scatter(summed_a, "fsdp", scatter_dimension=0, tiled=True),
        lax.psum_scatter(summed_b, "fsdp", scatter_dimension=0, tiled=True),
    )
    return (part_a, part_b, pair_loss_total.reshape(1), reward_margin.reshape(1))


def solution(mesh):
    placed = (
        P("dp", None, "fsdp", None),
        P("dp", None, "fsdp", None),
        P("dp", None, "fsdp"),
        P("fsdp", None),
        P("fsdp", None),
        P(),
    )
    return jax.shard_map(
        shards,
        mesh=mesh,
        in_specs=placed,
        out_specs=(P("fsdp", None), P("fsdp", None), P("dp"), P("dp")),
        check_vma=False,
    )
```

profile of v0, /device:TPU:0, one launch (start us, length us, event | category | flops | bytes accessed | tf_op | source)
XLA Modules:
  0.0 385.1 jit_solution(14346829637452022553)
XLA Ops:
  7.2 0.0 copy-start
  7.2 0.0 all-gather.5.cloned.1.call-start
  7.2 0.7 all-gather.5.cloned.1.call-update
  7.9 0.0 all-gather.3.cloned.1.call-start
  8.0 0.7 all-gather.3.cloned.1.call-update
  8.7 0.0 reduce-scatter.3.cloned.1.call-start
  8.7 44.4 %all-gather.5.cloned.1.call-done = bf16[8192,64]{0,1:T(8,128)(2,1)} async-done(((bf16[1024,64]{0,1:T(8,128)(2,1)}), bf16[8192,64]{0,1:T(8,128)(2,1)}) %all-gather.5.cloned.1.call-update) | async-done | bytes 1048592 | tf_op jit(solution)/shard_map/all_gather | solution.py:22
  53.1 3.9 %convolution_convert_fusion = bf16[256,64]{0,1:T(8,128)(2,1)S(1)} fusion(bf16[256,8192]{1,0:T(8,128)(2,1)} %bitcast.31, bf16[8192,64]{0,1:T(8,128)(2,1)} %all-gather.5.cloned.1.call-done), kind=kOutput, calls=%fused_computation.7 | convolution fusion | flops 268451840 | bytes 5275648 | tf_op jit(solution)/shard_map/dot_general | solution.py:20
  57.0 0.0 copy-start.1
  57.0 0.0 copy-start.2
  57.0 0.0 copy-start.3
  57.0 121.9 %all-gather.3.cloned.1.call-done = bf16[8192,512]{1,0:T(8,128)(2,1)} async-done(((bf16[1024,512]{1,0:T(8,128)(2,1)}), bf16[8192,512]{1,0:T(8,128)(2,1)}) %all-gather.3.cloned.1.call-update) | async-done | bytes 8388624 | tf_op jit(solution)/shard_map/all_gather | solution.py:17
  179.0 7.0 %fusion.10 = f32[256,512]{1,0:T(8,128)S(1)} fusion(bf16[256,8192]{1,0:T(8,128)(2,1)} %bitcast.32, bf16[8192,512]{1,0:T(8,128)(2,1)} %all-gather.3.cloned.1.call-done), kind=kOutput, calls=%fused_computation.20 | convolution fusion | flops 2147483648 | bytes 13107200 | tf_op jit(solution)/shard_map/dot_general | solution.py:15
  185.9 0.0 copy-done
  186.0 0.0 copy-done.1
  186.0 0.4 fusion.3
  186.4 0.0 copy-done.2
  186.4 0.1 fusion.7
  186.5 18.4 %psum.21 = f32[2]{0:T(128)S(1)} all-reduce(f32[2]{0:T(128)S(1)} %fusion.7), channel_id=1, replica_groups=mesh['dp'=4,'fsdp'=8] {'fsdp'}, use_global_device_ids=true, to_apply=%region_2.0 | all-reduce | flops 2 | bytes 16 | tf_op jit(solution)/shard_map/psum | solution.py:35
  204.9 0.6 fusion.9
  206.9 0.0 copy-done.3
  206.9 0.1 bitcast_multiply_fusion
  207.0 0.1 fusion.5
  207.1 4.7 %convolution_bitcast_fusion = f32[8192,64]{0,1:T(8,128)} fusion(bf16[256,8192]{1,0:T(8,128)(2,1)} %bitcast.33, bf16[256,512]{1,0:T(8,128)(2,1)S(1)} %fusion.5, bf16[64,512]{1,0:T(8,128)(2,1)S(1)} %copy-done), kind=kOutput, calls=%fused_computation | convolution fusion | flops 285245440 | bytes 6619136 | tf_op jit(solution)/shard_map/dot_general | solution.py:59
  211.8 0.0 reduce-scatter.3.cloned.1.call-update
  211.9 0.0 reduce-scatter.5.cloned.1.call-start
  211.9 1.0 convolution_multiply_fusion.1
  212.9 0.0 reduce-scatter.5.cloned.1.call-update
  212.9 0.0 all-reduce.2.cloned.1.call-start
  213.0 64.4 %reduce-scatter.3.cloned.1.call-done = f32[1024,64]{0,1:T(8,128)} async-done(((f32[8192,64]{0,1:T(8,128)}), f32[1024,64]{0,1:T(8,128)}) %reduce-scatter.3.cloned.1.call-update) | async-done | bytes 262160 | tf_op jit(solution)/shard_map/reduce_scatter | solution.py:67
  277.4 0.0 all-reduce.2.cloned.1.call-update
  277.5 63.9 %reduce-scatter.5.cloned.1.call-done = f32[64,64]{1,0:T(8,128)} async-done(((f32[512,64]{1,0:T(8,128)}), f32[64,64]{1,0:T(8,128)}) %reduce-scatter.5.cloned.1.call-update) | async-done | bytes 16400 | tf_op jit(solution)/shard_map/reduce_scatter | solution.py:68
  341.4 11.5 %psum.25 = f32[64,64]{1,0:T(8,128)} all-reduce(f32[64,64]{1,0:T(8,128)} %reduce-scatter.5.cloned.1.call-done), channel_id=1, replica_groups=mesh['dp'=4,'fsdp'=8] {'dp'}, use_global_device_ids=true, to_apply=%region_5.6 | all-reduce | flops 4096 | bytes 32768 | tf_op jit(solution)/shard_map/psum | solution.py:65
  352.9 21.7 %all-reduce.2.cloned.1.call-done = f32[1024,64]{0,1:T(8,128)} async-done(((f32[1024,64]{0,1:T(8,128)}), f32[1024,64]{0,1:T(8,128)}) %all-reduce.2.cloned.1.call-update) | async-done | bytes 262160 | tf_op jit(solution)/shard_map/psum | solution.py:65
  374.6 1.7 copy.12
  (1 shorter events, 0.0 us)
Async XLA Ops:
  7.2 178.8 %copy-start = (bf16[64,512]{1,0:T(8,128)(2,1)S(1)}, bf16[64,512]{1,0:T(8,128)(2,1)}, u32[]{:S(2)}) copy-start(bf16[64,512]{1,0:T(8,128)(2,1)} %param.12) | copy-start | bytes 196612
  7.2 45.9 %all-gather.5.cloned.1.call-start = ((), (), s32[]{:S(2)}) async-start(), calls=%async_computation.3 | async-start | bytes 1179648 | tf_op jit(solution)/shard_map/all_gather | solution.py:22
  7.9 171.1 %all-gather.3.cloned.1.call-start = ((), (), s32[]{:S(2)}) async-start(), calls=%async_computation.2 | async-start | bytes 9437184 | tf_op jit(solution)/shard_map/all_gather | solution.py:17
  8.7 268.7 %reduce-scatter.3.cloned.1.call-start = ((), (), s32[]{:S(2)}) async-start(), calls=%async_computation.4 | async-start | bytes 2359296 | tf_op jit(solution)/shard_map/reduce_scatter | solution.py:67
  57.0 129.0 %copy-start.1 = (bf16[1,2,128,512]{3,2,1,0:T(8,128)(2,1)S(1)}, bf16[1,2,128,512]{3,2,1,0:T(8,128)(2,1)}, u32[]{:S(2)}) copy-start(bf16[1,2,128,512]{3,2,1,0:T(8,128)(2,1)} %param.8) | copy-start | bytes 786436
  57.0 129.3 %copy-start.2 = (s32[1,2,128]{2,1,0:T(2,128)S(1)}, s32[1,2,128]{2,1,0:T(2,128)}, u32[]{:S(2)}) copy-start(s32[1,2,128]{2,1,0:T(2,128)} %param.9) | copy-start | bytes 3076
  57.0 149.8 %copy-start.3 = (f32[2]{0:T(128)S(1)}, f32[2]{0:T(128)}, u32[]{:S(2)}) copy-start(f32[2]{0:T(128)} %constant.19.clone) | copy-start | bytes 28
  211.9 129.5 %reduce-scatter.5.cloned.1.call-start = ((), (), s32[]{:S(2)}) async-start(), calls=%async_computation.6 | async-start | bytes 294912 | tf_op jit(solution)/shard_map/reduce_scatter | solution.py:68
  212.9 161.7 %all-reduce.2.cloned.1.call-start = ((), (), s32[]{:S(2)}) async-start(), calls=%async_computation.5 | async-start | bytes 524288 | tf_op jit(solution)/shard_map/psum | solution.py:65
Sparse Core Ops, SparseCore 0:
  10.2 42.8 all-gather.4
  55.3 123.6 all-gather.2
  212.0 65.3 reduce-scatter.2
  281.1 60.2 reduce-scatter.4
  343.6 30.9 all-reduce.1
where the time goes:
time: 385 us
  waiting for transfers between devices  318 us (83%)
  blocking collectives  29.9 us (8%)
  between operations  17.6 us (5%)
  matrix products  16.9 us (4%)
    all_gather x1, waiting for transfers between devices, shards(): lax.all_gather(value_matrix, 'fsdp', axis=0, tiled=True)  122 us
    reduce_scatter x1, waiting for transfers between devices, shards(): lax.psum_scatter(summed_a, 'fsdp', scatter_dimension=0, tiled=True)  64.4 us
    reduce_scatter x1, waiting for transfers between devices, shards(): lax.psum_scatter(summed_b, 'fsdp', scatter_dimension=0, tiled=True)  63.9 us
    all_gather x1, waiting for transfers between devices, shards(): lax.all_gather(adapter_down, 'fsdp', axis=0, tiled=True)  44.4 us
    psum x1, waiting for transfers between devices, shards(): summed_a, summed_b = lax.psum((down_gradient, up_gradient_flipped), 'dp')  21.7 us
    psum x1, blocking collectives, shards(): ratio = lax.psum(partial_value, 'fsdp')  18.4 us
    psum x1, blocking collectives, shards(): summed_a, summed_b = lax.psum((down_gradient, up_gradient_flipped), 'dp')  11.5 us
  transfers between devices with their start and end apart: 5, of which 5 were waited for; matrix products, arithmetic and copies ran while one was open for 1% of the time, Pallas kernels for 0%

commit v1 on v0

v1 whole, which is shorter than its diff:
```python
import functools

import jax
import jax.numpy as jnp
from jax import lax
from jax.experimental import pallas as pl
from jax.experimental.pallas import tpu as pltpu
from jax.sharding import PartitionSpec as P

DPO_BETA = 0.5
ADAPTER_SCALE = 2.0
LANES = 128
PACK = 128
PIECES = 6
MESH = pl.DeviceIdType.MESH


def kernel(
    n_dp, n_fsdp,
    hid_hbm, read_hbm, resp_ref, value_hbm, down_ref, up_ref,
    down_out, up_out, loss_out, margin_out,
    hid, read, weights, base, acc_l, acc_r, t_pol, grad_low_t,
    ratio_buf, part, buf1, send2, buf2, total2, send3, buf3, final,
    local_sem, ring_s, ring_r, x_s, x_r, core_s, core_r,
    ratio_s, ratio_r, s1, r1, s2, r2, s3, r3, s4, r4,
):
    half = n_fsdp // 2
    rows = value_hbm.shape[0]
    rank = down_ref.shape[1]
    tokens = hid.shape[0]
    seq = tokens // 2
    piece_rows = weights.shape[1] // PIECES
    groups = rows // PACK
    up_rows = base.shape[1] // n_fsdp

    me = lax.axis_index("fsdp")
    d = lax.axis_index("dp")
    core = lax.rem(d, 2)
    xbit = lax.rem(lax.div(d, 2), 2)
    core_peer = d + 1 - 2 * core
    x_peer = d + 2 - 4 * xbit

    col, row = lax.rem(me, 2), lax.div(me, 2)
    pos = row * (1 - col) + (n_fsdp - 1 - row) * col

    def at(p):
        p = lax.rem(p + 2 * n_fsdp, n_fsdp)
        c = lax.div(p, half)
        r = p * (1 - c) + (n_fsdp - 1 - p) * c
        return 2 * r + c

    ring_peer = (at(pos + 1), at(pos - 1))

    def shard_of(way, s):
        return at(pos - s) if way == 0 else at(pos + s)

    def piece(q, p):
        return weights.at[q, pl.ds(pl.multiple_of(p * piece_rows, piece_rows), piece_rows), :]

    own = (xbit * 2 + core, 4 + core)
    x_own = (1 - xbit) * 2 + core
    core_own = (xbit * 2 + 1 - core, 4 + 1 - core, (1 - xbit) * 2 + 1 - core)

    def remote(src, dst, send, recv, **where):
        return pltpu.make_async_remote_copy(
            src_ref=src, dst_ref=dst, send_sem=send, recv_sem=recv,
            device_id=where, device_id_type=MESH,
        )

    def ring_copy(way, s, kind, q):
        ref = piece(q, own[kind])
        return remote(ref, ref, ring_s.at[way, s - 1, kind], ring_r.at[way, s - 1, kind], fsdp=ring_peer[way])

    def x_copy(way, s, q, p):
        ref = piece(q, p)
        return remote(ref, ref, x_s.at[way, s - 1], x_r.at[way, s - 1], dp=x_peer)

    def core_copy(way, s, kind, q, p):
        ref = piece(q, p)
        return remote(ref, ref, core_s.at[way, s - 1, kind], core_r.at[way, s - 1, kind], dp=core_peer)

    def has(way, s, kind):
        return s < half or (s == half and way == kind)

    value_copy = pltpu.make_async_copy(value_hbm, weights.at[me, pl.ds(0, rows), :], local_sem.at[0])
    hid_copy = pltpu.make_async_copy(hid_hbm, hid, local_sem.at[1])
    read_copy = pltpu.make_async_copy(read_hbm, read, local_sem.at[2])
    value_copy.start()
    hid_copy.start()
    read_copy.start()

    barrier = pltpu.get_barrier_semaphore()

    def greet_fsdp(k, _):
        pl.semaphore_signal(barrier, inc=1, device_id={"fsdp": lax.rem(me + k, n_fsdp)}, device_id_type=MESH)
        return 0

    def greet_dp(k, _):
        pl.semaphore_signal(barrier, inc=1, device_id={"dp": lax.rem(d + k, n_dp)}, device_id_type=MESH)
        return 0

    lax.fori_loop(1, n_fsdp, greet_fsdp, 0)
    lax.fori_loop(1, n_dp, greet_dp, 0)

    packed = [down_ref[g * PACK:(g + 1) * PACK, :] for g in range(groups)]
    width = weights.shape[2]
    if groups * rank < width:
        packed.append(jnp.zeros((PACK, width - groups * rank), jnp.bfloat16))
    weights[me, pl.ds(rows, PACK), :] = jnp.concatenate(packed, axis=1)

    value_copy.wait()
    pl.semaphore_wait(barrier, n_fsdp + n_dp - 2)

    for kind in (0, 1):
        for way in (0, 1):
            if has(way, 1, kind):
                ring_copy(way, 1, kind, me).start()

    def multiply(q):
        first = pl.multiple_of(q * rows, rows)
        base[...] += jnp.dot(
            hid[:, pl.ds(first, rows)], weights[q, 0:rows, :], preferred_element_type=jnp.float32
        )
        left, right = acc_l[...], acc_r[...]
        for t in range(groups // 2):
            tile = weights[q, rows:rows + PACK, t * LANES:(t + 1) * LANES]
            begin = pl.multiple_of(q * rows + 2 * t * PACK, PACK)
            left += jnp.dot(hid[:, pl.ds(begin, PACK)], tile, preferred_element_type=jnp.float32)
            begin = pl.multiple_of(q * rows + (2 * t + 1) * PACK, PACK)
            right += jnp.dot(hid[:, pl.ds(begin, PACK)], tile, preferred_element_type=jnp.float32)
        acc_l[...] = left
        acc_r[...] = right

    base[...] = jnp.zeros_like(base)
    acc_l[...] = jnp.zeros_like(acc_l)
    acc_r[...] = jnp.zeros_like(acc_r)
    hid_copy.wait()
    multiply(me)

    def take_ring(s, kind):
        for way in (0, 1):
            if has(way, s, kind):
                q = shard_of(way, s)
                ring_copy(way, s, kind, q).wait_recv()
                if has(way, s + 1, kind):
                    ring_copy(way, s + 1, kind, q).start()
                if kind == 0:
                    x_copy(way, s, q, own[0]).start()
                core_copy(way, s, kind, q, own[kind]).start()

    def take_x(s):
        for way in (0, 1):
            if has(way, s, 0):
                q = shard_of(way, s)
                x_copy(way, s, q, x_own).wait_recv()
                core_copy(way, s, 2, q, x_own).start()

    def finish(s):
        for way in (0, 1):
            for kind in (0, 1, 2):
                if has(way, s, kind % 2):
                    core_copy(way, s, kind, shard_of(way, s), core_own[kind]).wait_recv()
        if s == half:
            multiply(shard_of(0, s))
        else:
            def both(i, _):
                multiply(at(pos + s * (2 * i - 1)))
                return 0
            lax.fori_loop(0, 2, both, 0)

    for s in range(1, half + 1):
        take_ring(s, 0)
        if s > 1:
            take_x(s - 1)
        take_ring(s, 1)
        if s > 1:
            finish(s - 1)
    take_x(half)
    finish(half)

    low = (acc_l[:, 0:rank] + acc_r[:, rank:2 * rank]).astype(jnp.bfloat16)
    ref_act = base[...]
    policy = ref_act + ADAPTER_SCALE * jnp.dot(low, up_ref[...], preferred_element_type=jnp.float32)
    t_policy = jnp.tanh(policy)
    t_pol[...] = t_policy
    read_copy.wait()
    resp = resp_ref[...].astype(jnp.float32)
    masks = [
        jnp.transpose(jnp.broadcast_to(resp[i:i + 1, :], (seq, seq)))[:, 0:1] for i in (0, 1)
    ]
    mask = jnp.concatenate(masks, axis=0)
    weighted = read[...].astype(jnp.float32) * mask
    scores = weighted * (t_policy - jnp.tanh(ref_act))
    diff = scores[0:seq, :] - scores[seq:, :]
    tile = jnp.zeros((seq, LANES), jnp.float32)
    for t in range(diff.shape[1] // LANES):
        tile += diff[:, t * LANES:(t + 1) * LANES]
    ratio_buf[me] = jnp.sum(tile.reshape(seq // 8, 8, LANES), axis=0)

    def ratio_copy(k):
        return remote(
            ratio_buf.at[me], ratio_buf.at[me], ratio_s.at[k], ratio_r.at[k], fsdp=lax.rem(me + k, n_fsdp)
        )

    def each(first, last, body):
        def step(k, _):
            body(k)
            return 0
        lax.fori_loop(first, last, step, 0)

    each(1, n_fsdp, lambda k: ratio_copy(k).start())
    base[...] = weighted * (1.0 - t_policy * t_policy)
    each(1, n_fsdp, lambda k: ratio_copy(k).wait())

    margin = DPO_BETA * jnp.sum(jnp.sum(ratio_buf[...], axis=0), keepdims=True)
    loss = jnp.maximum(-margin, 0.0) + jnp.log1p(jnp.exp(-jnp.abs(margin)))
    gate = 1.0 / (1.0 + jnp.exp(margin))
    loss_out[...] = jnp.broadcast_to(loss, loss_out.shape)
    margin_out[...] = jnp.broadcast_to(margin, margin_out.shape)
    coef = DPO_BETA * gate
    grad_h = jnp.concatenate(
        [(-coef * base[0:seq, :]).astype(jnp.bfloat16), (coef * base[seq:, :]).astype(jnp.bfloat16)], axis=0
    )
    grad_low = ADAPTER_SCALE * lax.dot_general(
        grad_h, up_ref[...], (((1,), (1,)), ((), ())), preferred_element_type=jnp.float32
    )
    grad_low_t[...] = jnp.transpose(grad_low).astype(jnp.bfloat16)
    grad_b_t = ADAPTER_SCALE * lax.dot_general(
        grad_h, low, (((0,), (0,)), ((), ())), preferred_element_type=jnp.float32
    )
    for q in range(n_fsdp):
        block = grad_b_t[q * up_rows:(q + 1) * up_rows, :]
        block = jnp.concatenate([block, jnp.zeros((up_rows, LANES - rank), jnp.float32)], axis=1)
        if up_rows < rank:
            block = jnp.concatenate([block, jnp.zeros((rank - up_rows, LANES), jnp.float32)], axis=0)
        part[q, :, rows:rows + LANES] = block

    half_rows, quarter = rank // 2, rank // 4
    mine1 = pl.multiple_of(core * half_rows, half_rows)
    theirs1 = pl.multiple_of((1 - core) * half_rows, half_rows)

    def block_of(k):
        return lax.rem(me + k, n_fsdp)

    def copy1(k):
        return remote(
            part.at[block_of(k), pl.ds(theirs1, half_rows), :], buf1.at[k], s1.at[k], r1.at[k], dp=core_peer
        )

    def copy2(k):
        return remote(send2.at[k], buf2.at[k], s2.at[k], r2.at[k], dp=x_peer)

    def copy3(k):
        return remote(send3.at[k], buf3.at[k], s3.at[k], r3.at[k], fsdp=block_of(k))

    def stage1(k):
        q = block_of(k)
        part[q, :, 0:rows] = jnp.dot(
            grad_low_t[...], hid[:, pl.ds(pl.multiple_of(q * rows, rows), rows)],
            preferred_element_type=jnp.float32,
        )
        copy1(k).start()

    def stage2(k):
        q = block_of(k)
        copy1(k).wait_recv()
        give = pl.multiple_of((1 - xbit) * quarter, quarter)
        keep = pl.multiple_of(xbit * quarter, quarter)
        send2[k] = (part[q, pl.ds(mine1 + give, quarter), :] + buf1[k, pl.ds(give, quarter), :]).astype(jnp.bfloat16)
        copy2(k).start()
        total2[k] = part[q, pl.ds(mine1 + keep, quarter), :] + buf1[k, pl.ds(keep, quarter), :]

    def stage3(k):
        copy2(k).wait_recv()
        send3[k] = (total2[k] + buf2[k].astype(jnp.float32)).astype(jnp.bfloat16)
        copy3(k).start()

    each(1, n_fsdp, stage1)
    stage1(0)
    each(1, n_fsdp, stage2)
    stage2(0)
    each(1, n_fsdp, stage3)
    copy2(0).wait_recv()
    total2[0] = total2[0] + buf2[0].astype(jnp.float32)

    def stage4(k):
        copy3(k).wait_recv()
        total2[0] = total2[0] + buf3[k].astype(jnp.float32)

    each(1, n_fsdp, stage4)
    final[0] = total2[0]

    def copy4(k):
        return remote(final.at[0], final.at[k], s4.at[k], r4.at[k], dp=lax.rem(d + k, n_dp))

    each(1, n_dp, lambda k: copy4(k).start())

    for s in range(1, half + 1):
        for way in (0, 1):
            for kind in (0, 1):
                if has(way, s, kind):
                    ring_copy(way, s, kind, me).wait_send()
                    core_copy(way, s, kind, me, own[kind]).wait_send()
            if has(way, s, 0):
                x_copy(way, s, me, own[0]).wait_send()
                core_copy(way, s, 2, me, x_own).wait_send()
    each(0, n_fsdp, lambda k: copy1(k).wait_send())
    each(0, n_fsdp, lambda k: copy2(k).wait_send())
    each(1, n_fsdp, lambda k: copy3(k).wait_send())

    each(1, n_dp, lambda k: copy4(k).wait())
    for c in (0, 1):
        for x in (0, 1):
            begin = c * half_rows + x * quarter
            total = jnp.zeros((quarter, rows + LANES), jnp.float32)
            for h in range(n_dp // 4):
                slot = lax.rem(d - (h * 4 + x * 2 + c) + n_dp, n_dp)
                total += final[slot]
            down_out[begin:begin + quarter, :] = total[:, 0:rows]
            up_out[begin:begin + quarter, :] = total[:, rows:rows + LANES]


def shards(n_dp, n_fsdp, hidden_input, readout, response, value_matrix, adapter_down, adapter_up):
    seq = hidden_input.shape[2]
    tokens = 2 * seq
    model = hidden_input.shape[3]
    rows, features = value_matrix.shape
    rank = adapter_down.shape[1]
    half = n_fsdp // 2
    quarter = rank // 4
    wide = rows + LANES
    f32, bf16 = jnp.float32, jnp.bfloat16
    vmem = pl.BlockSpec(memory_space=pltpu.VMEM)
    hbm = pl.BlockSpec(memory_space=pl.ANY)
    dma = pltpu.SemaphoreType.DMA
    outs = pl.pallas_call(
        functools.partial(kernel, n_dp, n_fsdp),
        out_shape=(
            jax.ShapeDtypeStruct((rank, rows), f32),
            jax.ShapeDtypeStruct((rank, LANES), f32),
            jax.ShapeDtypeStruct((8, LANES), f32),
            jax.ShapeDtypeStruct((8, LANES), f32),
        ),
        in_specs=[hbm, hbm, vmem, hbm, vmem, vmem],
        out_specs=(vmem, vmem, vmem, vmem),
        scratch_shapes=[
            pltpu.VMEM((tokens, model), bf16),
            pltpu.VMEM((tokens, features), bf16),
            pltpu.VMEM((n_fsdp, rows + PACK, features), bf16),
            pltpu.VMEM((tokens, features), f32),
            pltpu.VMEM((tokens, LANES), f32),
            pltpu.VMEM((tokens, LANES), f32),
            pltpu.VMEM((tokens, features), f32),
            pltpu.VMEM((rank, tokens), bf16),
            pltpu.VMEM((n_fsdp, 8, LANES), f32),
            pltpu.VMEM((n_fsdp, rank, wide), f32),
            pltpu.VMEM((n_fsdp, rank // 2, wide), f32),
            pltpu.VMEM((n_fsdp, quarter, wide), bf16),
            pltpu.VMEM((n_fsdp, quarter, wide), bf16),
            pltpu.VMEM((n_fsdp, quarter, wide), f32),
            pltpu.VMEM((n_fsdp, quarter, wide), bf16),
            pltpu.VMEM((n_fsdp, quarter, wide), bf16),
            pltpu.VMEM((n_dp, quarter, wide), f32),
            dma((3,)),
            dma((2, half, 2)), dma((2, half, 2)),
            dma((2, half)), dma((2, half)),
            dma((2, half, 3)), dma((2, half, 3)),
            dma((n_fsdp,)), dma((n_fsdp,)),
            dma((n_fsdp,)), dma((n_fsdp,)),
            dma((n_fsdp,)), dma((n_fsdp,)),
            dma((n_fsdp,)), dma((n_fsdp,)),
            dma((n_dp,)), dma((n_dp,)),
        ],
        compiler_params=pltpu.CompilerParams(
            collective_id=0, has_side_effects=True, vmem_limit_bytes=56 << 20
        ),
        name="dpo_adapter_gradient",
    )(
        hidden_input.reshape(tokens, model),
        readout.reshape(tokens, features),
        response.reshape(2, seq),
        value_matrix,
        adapter_down,
        adapter_up,
    )
    down_t, up_block, loss, margin = outs
    return (
        down_t.T,
        up_block[:features // n_fsdp, :rank],
        loss[0, :1],
        margin[0, :1],
    )


def solution(mesh):
    placed = (
        P("dp", None, "fsdp", None),
        P("dp", None, "fsdp", None),
        P("dp", None, "fsdp"),
        P("fsdp", None),
        P("fsdp", None),
        P(),
    )
    return jax.shard_map(
        functools.partial(shards, mesh.shape["dp"], mesh.shape["fsdp"]),
        mesh=mesh,
        in_specs=placed,
        out_specs=(P("fsdp", None), P("fsdp", None), P("dp"), P("dp")),
        check_vma=False,
    )
```

time: 385 us -> 75.9 us (0.20)
  waiting for transfers between devices: 318 us -> 0 us
  Pallas kernels: 0 us -> 67.2 us
  blocking collectives: 29.9 us -> 0 us
  between operations: 17.6 us -> 0.64 us
  matrix products: 16.9 us -> 0 us
  local copies, waits for them, and re-layouts: 2.28 us -> 7.17 us
    all_gather x2 -> x0, waiting for transfers between devices: 166 us -> none  [the longest x1 122 us: shards(): lax.all_gather(value_matrix, 'fsdp', axis=0, tiled=True)]
    reduce_scatter x2 -> x0, waiting for transfers between devices: 128 us -> none  [the longest x1 64.4 us: shards(): lax.psum_scatter(summed_a, 'fsdp', scatter_dimension=0, tiled=True)]
    pallas_call x0 -> x1, Pallas kernels: none -> 67.2 us  [shards(): pl.pallas_call(functools.partial(kernel, n_dp, n_fsdp), out_shape=(jax.Sh...]
    psum x2 -> x0, blocking collectives: 29.9 us -> none  [the longest x1 18.4 us: shards(): ratio = lax.psum(partial_value, 'fsdp')]
    psum x1 -> x0, waiting for transfers between devices: 21.7 us -> none  [shards(): summed_a, summed_b = lax.psum((down_gradient, up_gradient_flipped), 'dp')]
    dot_general x5 -> x0, matrix products: 16.9 us -> none  [the longest x1 6.97 us: shards(): jnp.dot(token_row_block, lax.all_gather(value_matrix, 'fsdp', axis=0, til...]
  transfers between devices with their start and end apart: 5 -> 0, of which waited for: 5 -> 0; matrix products, arithmetic and copies ran while one was open for 1% -> 0% of each run, Pallas kernels for 0% -> 0%
where the time goes in v1:
time: 75.9 us; the launch traced here: 75 us
  Pallas kernels  67.2 us (89%)
  local copies, waits for them, and re-layouts  7.17 us (9%)
    pallas_call x1, Pallas kernels, shards(): pl.pallas_call(functools.partial(kernel, n_dp, n_fsdp), out_shape=(jax.Sh...  67.2 us
    unnamed x3, local copies, waits for them, and re-layouts  4.79 us

profile of v1, /device:TPU:0, one launch (start us, length us, event | category | flops | bytes accessed | tf_op | source)
XLA Modules:
  0.0 75.0 jit_solution(9811578205381377481)
XLA Ops:
  0.6 1.7 %copy.10.down_ref = bf16[1024,64]{1,0:T(8,128)(2,1)} copy(bf16[1024,64]{0,1:T(8,128)(2,1)} %param.10) | data formatting | bytes 262144 | tf_op args[4]
  2.4 67.2 %dpo_adapter_gradient.1 = (f32[64,1024]{1,0:T(8,128)}, f32[64,128]{1,0:T(8,128)}, f32[8,128]{1,0:T(8,128)}, f32[8,128]{1,0:T(8,128)}) custom-call(bf16[256,8192]{1,0:T(8,128)(2,1)} %bitcast.7, bf16[256,512]{1,0:T(8,128)(2,1)} %bitcast.8, s32[2,128]{1,0:T(2,128)} %bitcast.11, bf16[1024,512]{1,0:T(8,128)(2,1)} %value_hbm.1, bf16[1024,64]{1,0:T(8,128)(2,1)} %copy.10.down_ref, ...), custom_call_target="tpu_custom_call" | custom-call | tf_op jit(solution)/shard_map/dpo_adapter_gradient/pallas_call | solution.py:336
  69.6 1.2 %slice.11 = f32[1,1]{1,0:T(1,128)} slice(f32[8,128]{1,0:T(8,128)} %get-tuple-element.11), slice={[0:1], [0:1]} | slice | bytes 8 | tf_op jit(solution)/shard_map/slice | solution.py:391
  70.8 1.2 %slice.10 = f32[1,1]{1,0:T(1,128)} slice(f32[8,128]{1,0:T(8,128)} %get-tuple-element.10), slice={[0:1], [0:1]} | slice | bytes 8 | tf_op jit(solution)/shard_map/slice | solution.py:390
  72.0 1.7 %copy.13 = f32[1024,64]{0,1:T(8,128)} copy(f32[1024,64]{0,1:T(8,128)} %bitcast.9) | data formatting | bytes 524288
  73.7 1.4 %copy.14 = f32[64,64]{1,0:T(8,128)} copy(f32[64,64]{1,0:T(8,128)} %bitcast.10) | data formatting | bytes 32768

commit v2 on v1

--- a/solution.py
+++ b/solution.py
@@ -11,25 +11,25 @@
 ADAPTER_SCALE = 2.0
 LANES = 128
 PACK = 128
-PIECES = 6
 MESH = pl.DeviceIdType.MESH
 
 
 def kernel(
     n_dp, n_fsdp,
     hid_hbm, read_hbm, resp_ref, value_hbm, down_ref, up_ref,
-    down_out, up_out, loss_out, margin_out,
-    hid, read, weights, base, acc_l, acc_r, t_pol, grad_low_t,
+    out,
+    hid, read, weights, base, acc_l, acc_r, grad_low_t,
     ratio_buf, part, buf1, send2, buf2, total2, send3, buf3, final,
     local_sem, ring_s, ring_r, x_s, x_r, core_s, core_r,
     ratio_s, ratio_r, s1, r1, s2, r2, s3, r3, s4, r4,
 ):
     half = n_fsdp // 2
     rows = value_hbm.shape[0]
-    rank = down_ref.shape[1]
+    rank = down_ref.shape[0]
     tokens = hid.shape[0]
     seq = tokens // 2
-    piece_rows = weights.shape[1] // PIECES
+    swapped = weights.shape[1] * 11 // 72 // 16 * 16
+    kept = (weights.shape[1] - 4 * swapped) // 2
     groups = rows // PACK
     up_rows = base.shape[1] // n_fsdp
 
@@ -54,12 +54,14 @@
     def shard_of(way, s):
         return at(pos - s) if way == 0 else at(pos + s)
 
-    def piece(q, p):
-        return weights.at[q, pl.ds(pl.multiple_of(p * piece_rows, piece_rows), piece_rows), :]
-
-    own = (xbit * 2 + core, 4 + core)
+    def piece(q, kind, p):
+        if kind == 1:
+            return weights.at[q, pl.ds(pl.multiple_of(4 * swapped + p * kept, 16), kept), :]
+        return weights.at[q, pl.ds(pl.multiple_of(p * swapped, 16), swapped), :]
+
+    own = (xbit * 2 + core, core)
     x_own = (1 - xbit) * 2 + core
-    core_own = (xbit * 2 + 1 - core, 4 + 1 - core, (1 - xbit) * 2 + 1 - core)
+    core_own = (xbit * 2 + 1 - core, 1 - core, (1 - xbit) * 2 + 1 - core)
 
     def remote(src, dst, send, recv, **where):
         return pltpu.make_async_remote_copy(
@@ -68,15 +70,15 @@
         )
 
     def ring_copy(way, s, kind, q):
-        ref = piece(q, own[kind])
+        ref = piece(q, kind, own[kind])
         return remote(ref, ref, ring_s.at[way, s - 1, kind], ring_r.at[way, s - 1, kind], fsdp=ring_peer[way])
 
     def x_copy(way, s, q, p):
-        ref = piece(q, p)
+        ref = piece(q, 0, p)
         return remote(ref, ref, x_s.at[way, s - 1], x_r.at[way, s - 1], dp=x_peer)
 
     def core_copy(way, s, kind, q, p):
-        ref = piece(q, p)
+        ref = piece(q, kind, p)
         return remote(ref, ref, core_s.at[way, s - 1, kind], core_r.at[way, s - 1, kind], dp=core_peer)
 
     def has(way, s, kind):
@@ -102,11 +104,13 @@
     lax.fori_loop(1, n_fsdp, greet_fsdp, 0)
     lax.fori_loop(1, n_dp, greet_dp, 0)
 
-    packed = [down_ref[g * PACK:(g + 1) * PACK, :] for g in range(groups)]
-    width = weights.shape[2]
-    if groups * rank < width:
-        packed.append(jnp.zeros((PACK, width - groups * rank), jnp.bfloat16))
-    weights[me, pl.ds(rows, PACK), :] = jnp.concatenate(packed, axis=1)
+    for t in range(groups // 2):
+        pair = [down_ref[:, g * PACK:(g + 1) * PACK].astype(jnp.float32) for g in (2 * t, 2 * t + 1)]
+        tile = jnp.transpose(jnp.concatenate(pair, axis=0)).astype(jnp.bfloat16)
+        weights[me, rows:rows + PACK, t * LANES:(t + 1) * LANES] = tile
+    used = groups // 2 * LANES
+    if used < weights.shape[2]:
+        weights[me, rows:rows + PACK, used:] = jnp.zeros((PACK, weights.shape[2] - used), jnp.bfloat16)
 
     value_copy.wait()
     pl.semaphore_wait(barrier, n_fsdp + n_dp - 2)
@@ -182,7 +186,6 @@
     ref_act = base[...]
     policy = ref_act + ADAPTER_SCALE * jnp.dot(low, up_ref[...], preferred_element_type=jnp.float32)
     t_policy = jnp.tanh(policy)
-    t_pol[...] = t_policy
     read_copy.wait()
     resp = resp_ref[...].astype(jnp.float32)
     masks = [
@@ -209,18 +212,8 @@
         lax.fori_loop(first, last, step, 0)
 
     each(1, n_fsdp, lambda k: ratio_copy(k).start())
-    base[...] = weighted * (1.0 - t_policy * t_policy)
-    each(1, n_fsdp, lambda k: ratio_copy(k).wait())
-
-    margin = DPO_BETA * jnp.sum(jnp.sum(ratio_buf[...], axis=0), keepdims=True)
-    loss = jnp.maximum(-margin, 0.0) + jnp.log1p(jnp.exp(-jnp.abs(margin)))
-    gate = 1.0 / (1.0 + jnp.exp(margin))
-    loss_out[...] = jnp.broadcast_to(loss, loss_out.shape)
-    margin_out[...] = jnp.broadcast_to(margin, margin_out.shape)
-    coef = DPO_BETA * gate
-    grad_h = jnp.concatenate(
-        [(-coef * base[0:seq, :]).astype(jnp.bfloat16), (coef * base[seq:, :]).astype(jnp.bfloat16)], axis=0
-    )
+    slope = DPO_BETA * weighted * (1.0 - t_policy * t_policy)
+    grad_h = jnp.concatenate([-slope[0:seq, :], slope[seq:, :]], axis=0).astype(jnp.bfloat16)
     grad_low = ADAPTER_SCALE * lax.dot_general(
         grad_h, up_ref[...], (((1,), (1,)), ((), ())), preferred_element_type=jnp.float32
     )
@@ -259,7 +252,6 @@
             grad_low_t[...], hid[:, pl.ds(pl.multiple_of(q * rows, rows), rows)],
             preferred_element_type=jnp.float32,
         )
-        copy1(k).start()
 
     def stage2(k):
         q = block_of(k)
@@ -275,8 +267,20 @@
         send3[k] = (total2[k] + buf2[k].astype(jnp.float32)).astype(jnp.bfloat16)
         copy3(k).start()
 
-    each(1, n_fsdp, stage1)
-    stage1(0)
+    each(0, n_fsdp, stage1)
+
+    each(1, n_fsdp, lambda k: ratio_copy(k).wait())
+    margin = DPO_BETA * jnp.sum(jnp.sum(ratio_buf[...], axis=0), keepdims=True)
+    loss = jnp.maximum(-margin, 0.0) + jnp.log1p(jnp.exp(-jnp.abs(margin)))
+    gate = 1.0 / (1.0 + jnp.exp(margin))
+
+    def send1(k):
+        q = block_of(k)
+        part[q] = part[q] * gate
+        copy1(k).start()
+
+    each(1, n_fsdp, send1)
+    send1(0)
     each(1, n_fsdp, stage2)
     stage2(0)
     each(1, n_fsdp, stage3)
@@ -316,8 +320,19 @@
             for h in range(n_dp // 4):
                 slot = lax.rem(d - (h * 4 + x * 2 + c) + n_dp, n_dp)
                 total += final[slot]
-            down_out[begin:begin + quarter, :] = total[:, 0:rows]
-            up_out[begin:begin + quarter, :] = total[:, rows:rows + LANES]
+            out[begin:begin + quarter, :] = total
+    wide = rows + LANES
+    out[rank:rank + 8, :] = jnp.broadcast_to(loss, (8, wide))
+    out[rank + 8:rank + 16, :] = jnp.broadcast_to(margin, (8, wide))
+
+
+def unpack(joined, down_out, up_out, loss_out, margin_out):
+    rank, rows = down_out.shape
+    up_rows = up_out.shape[0]
+    down_out[...] = joined[0:rank, 0:rows]
+    up_out[...] = joined[0:up_rows, rows:rows + up_out.shape[1]]
+    loss_out[0] = jnp.max(joined[rank:rank + 8, 0:LANES])
+    margin_out[0] = jnp.max(joined[rank + 8:rank + 16, 0:LANES])
 
 
 def shards(n_dp, n_fsdp, hidden_input, readout, response, value_matrix, adapter_down, adapter_up):
@@ -333,16 +348,11 @@
     vmem = pl.BlockSpec(memory_space=pltpu.VMEM)
     hbm = pl.BlockSpec(memory_space=pl.ANY)
     dma = pltpu.SemaphoreType.DMA
-    outs = pl.pallas_call(
+    joined = pl.pallas_call(
         functools.partial(kernel, n_dp, n_fsdp),
-        out_shape=(
-            jax.ShapeDtypeStruct((rank, rows), f32),
-            jax.ShapeDtypeStruct((rank, LANES), f32),
-            jax.ShapeDtypeStruct((8, LANES), f32),
-            jax.ShapeDtypeStruct((8, LANES), f32),
-        ),
+        out_shape=jax.ShapeDtypeStruct((rank + 16, wide), f32),
         in_specs=[hbm, hbm, vmem, hbm, vmem, vmem],
-        out_specs=(vmem, vmem, vmem, vmem),
+        out_specs=vmem,
         scratch_shapes=[
             pltpu.VMEM((tokens, model), bf16),
             pltpu.VMEM((tokens, features), bf16),
@@ -350,7 +360,6 @@
             pltpu.VMEM((tokens, features), f32),
             pltpu.VMEM((tokens, LANES), f32),
             pltpu.VMEM((tokens, LANES), f32),
-            pltpu.VMEM((tokens, features), f32),
             pltpu.VMEM((rank, tokens), bf16),
             pltpu.VMEM((n_fsdp, 8, LANES), f32),
             pltpu.VMEM((n_fsdp, rank, wide), f32),
@@ -380,16 +389,23 @@
         readout.reshape(tokens, features),
         response.reshape(2, seq),
         value_matrix,
-        adapter_down,
+        adapter_down.T,
         adapter_up,
     )
-    down_t, up_block, loss, margin = outs
-    return (
-        down_t.T,
-        up_block[:features // n_fsdp, :rank],
-        loss[0, :1],
-        margin[0, :1],
-    )
+    smem = pl.BlockSpec(memory_space=pltpu.SMEM)
+    down_t, up_block, loss, margin = pl.pallas_call(
+        unpack,
+        out_shape=(
+            jax.ShapeDtypeStruct((rank, rows), f32),
+            jax.ShapeDtypeStruct((features // n_fsdp, rank), f32),
+            jax.ShapeDtypeStruct((1,), f32),
+            jax.ShapeDtypeStruct((1,), f32),
+        ),
+        in_specs=[vmem],
+        out_specs=(vmem, vmem, smem, smem),
+        name="unpack_gradients",
+    )(joined)
+    return down_t.T, up_block, loss, margin
 
 
 def solution(mesh):

time: 75.9 us -> 68.7 us (0.905)
  local copies, waits for them, and re-layouts: 7.17 us -> 0 us
    unnamed x3 -> x0, local copies, waits for them, and re-layouts: 4.79 us -> none
    slice x2 -> x0, local copies, waits for them, and re-layouts: 2.38 us -> none  [the longest x1 1.19 us: shards(): margin[0, :1]]
    pallas_call x1 -> x2, Pallas kernels: 67.2 us -> 67.8 us  [the longest x1 66 us: shards(): pl.pallas_call(functools.partial(kernel, n_dp, n_fsdp), out_shape=jax.Sha...]
where the time goes in v2:
time: 68.7 us; the launch traced here: 68.4 us
  Pallas kernels  67.8 us (99%)
    pallas_call x1, Pallas kernels, shards(): pl.pallas_call(functools.partial(kernel, n_dp, n_fsdp), out_shape=jax.Sha...  66 us
    pallas_call x1, Pallas kernels, shards(): pl.pallas_call(unpack, out_shape=(jax.ShapeDtypeStruct((rank, rows), f32)...  1.72 us

profile of v2, /device:TPU:0, one launch (start us, length us, event | category | flops | bytes accessed | tf_op | source)
XLA Modules:
  0.0 68.4 jit_solution(2152133624741361958)
XLA Ops:
  0.6 66.0 %dpo_adapter_gradient.1.joined = f32[80,1152]{1,0:T(8,128)} custom-call(bf16[256,8192]{1,0:T(8,128)(2,1)} %bitcast.5, bf16[256,512]{1,0:T(8,128)(2,1)} %bitcast.6, s32[2,128]{1,0:T(2,128)} %bitcast.8, bf16[1024,512]{1,0:T(8,128)(2,1)} %value_hbm.1, bf16[64,1024]{1,0:T(8,128)(2,1)} %bitcast.7, bf16[64,512]{1,0:T(8,128)(2,1)} %up_ref.1), custom_call_target="tpu_custom_call" | custom-call | tf_op jit(solution)/shard_map/dpo_adapter_gradient/pallas_call | solution.py:351
  66.7 1.7 %unpack_gradients.1 = (f32[64,1024]{1,0:T(8,128)}, f32[64,64]{1,0:T(8,128)}, f32[1]{0:T(128)}, f32[1]{0:T(128)}) custom-call(f32[80,1152]{1,0:T(8,128)} %dpo_adapter_gradient.1.joined), custom_call_target="tpu_custom_call" | custom-call | tf_op jit(solution)/shard_map/unpack_gradients/pallas_call | solution.py:396

commit v3 on v2

--- a/solution.py
+++ b/solution.py
@@ -18,7 +18,7 @@
     n_dp, n_fsdp,
     hid_hbm, read_hbm, resp_ref, value_hbm, down_ref, up_ref,
     out,
-    hid, read, weights, base, acc_l, acc_r, grad_low_t,
+    hid, read, weighted, weights, base, acc_l, acc_r, grad_low_t,
     ratio_buf, part, buf1, send2, buf2, total2, send3, buf3, final,
     local_sem, ring_s, ring_r, x_s, x_r, core_s, core_r,
     ratio_s, ratio_r, s1, r1, s2, r2, s3, r3, s4, r4,
@@ -120,11 +120,20 @@
             if has(way, 1, kind):
                 ring_copy(way, 1, kind, me).start()
 
-    def multiply(q):
-        first = pl.multiple_of(q * rows, rows)
+    early = 4 * swapped // PACK * PACK
+
+    def multiply_early(q):
+        first = pl.multiple_of(q * rows, PACK)
         base[...] += jnp.dot(
-            hid[:, pl.ds(first, rows)], weights[q, 0:rows, :], preferred_element_type=jnp.float32
+            hid[:, pl.ds(first, early)], weights[q, 0:early, :], preferred_element_type=jnp.float32
         )
+
+    def multiply_late(q):
+        if early < rows:
+            first = pl.multiple_of(q * rows + early, PACK)
+            base[...] += jnp.dot(
+                hid[:, pl.ds(first, rows - early)], weights[q, early:rows, :], preferred_element_type=jnp.float32
+            )
         left, right = acc_l[...], acc_r[...]
         for t in range(groups // 2):
             tile = weights[q, rows:rows + PACK, t * LANES:(t + 1) * LANES]
@@ -139,61 +148,83 @@
     acc_l[...] = jnp.zeros_like(acc_l)
     acc_r[...] = jnp.zeros_like(acc_r)
     hid_copy.wait()
-    multiply(me)
-
-    def take_ring(s, kind):
-        for way in (0, 1):
-            if has(way, s, kind):
-                q = shard_of(way, s)
-                ring_copy(way, s, kind, q).wait_recv()
-                if has(way, s + 1, kind):
-                    ring_copy(way, s + 1, kind, q).start()
-                if kind == 0:
-                    x_copy(way, s, q, own[0]).start()
-                core_copy(way, s, kind, q, own[kind]).start()
-
-    def take_x(s):
-        for way in (0, 1):
-            if has(way, s, 0):
-                q = shard_of(way, s)
-                x_copy(way, s, q, x_own).wait_recv()
-                core_copy(way, s, 2, q, x_own).start()
-
-    def finish(s):
-        for way in (0, 1):
-            for kind in (0, 1, 2):
-                if has(way, s, kind % 2):
-                    core_copy(way, s, kind, shard_of(way, s), core_own[kind]).wait_recv()
-        if s == half:
-            multiply(shard_of(0, s))
-        else:
-            def both(i, _):
-                multiply(at(pos + s * (2 * i - 1)))
-                return 0
-            lax.fori_loop(0, 2, both, 0)
-
-    for s in range(1, half + 1):
-        take_ring(s, 0)
-        if s > 1:
-            take_x(s - 1)
-        take_ring(s, 1)
-        if s > 1:
-            finish(s - 1)
-    take_x(half)
-    finish(half)
-
-    low = (acc_l[:, 0:rank] + acc_r[:, rank:2 * rank]).astype(jnp.bfloat16)
-    ref_act = base[...]
-    policy = ref_act + ADAPTER_SCALE * jnp.dot(low, up_ref[...], preferred_element_type=jnp.float32)
-    t_policy = jnp.tanh(policy)
+    multiply_early(me)
+    multiply_late(me)
+
     read_copy.wait()
     resp = resp_ref[...].astype(jnp.float32)
     masks = [
         jnp.transpose(jnp.broadcast_to(resp[i:i + 1, :], (seq, seq)))[:, 0:1] for i in (0, 1)
     ]
-    mask = jnp.concatenate(masks, axis=0)
-    weighted = read[...].astype(jnp.float32) * mask
-    scores = weighted * (t_policy - jnp.tanh(ref_act))
+    weighted[...] = read[...].astype(jnp.float32) * jnp.concatenate(masks, axis=0)
+
+    def overtaken(way, s, kind):
+        return half >= 3 and way == 0 and s == half - 1 and kind == 1
+
+    def take_ring(way, s, kind):
+        if not has(way, s, kind):
+            return
+        q = shard_of(way, s)
+        ring_copy(way, s, kind, q).wait_recv()
+        if has(way, s + 1, kind) and not overtaken(way, s + 1, kind):
+            ring_copy(way, s + 1, kind, q).start()
+        if kind == 0 and overtaken(way, s, 1):
+            ring_copy(way, s, 1, shard_of(way, s - 1)).start()
+        if kind == 0:
+            x_copy(way, s, q, own[0]).start()
+        core_copy(way, s, kind, q, own[kind]).start()
+
+    def take_x(way, s):
+        if has(way, s, 0):
+            q = shard_of(way, s)
+            x_copy(way, s, q, x_own).wait_recv()
+            core_copy(way, s, 2, q, x_own).start()
+
+    def take_core(way, s, kind):
+        if has(way, s, kind % 2):
+            core_copy(way, s, kind, shard_of(way, s), core_own[kind]).wait_recv()
+
+    def finish_early(s):
+        for way in (0, 1):
+            take_core(way, s, 0)
+            take_core(way, s, 2)
+        for way in ((0, 1) if s < half else (0,)):
+            multiply_early(shard_of(way, s))
+
+    def finish_late(way, s):
+        take_core(way, s, 1)
+        multiply_late(shard_of(way, s))
+
+    for s in range(1, half):
+        for way in (0, 1):
+            take_ring(way, s, 0)
+        if s > 1:
+            for way in (0, 1):
+                take_x(way, s - 1)
+            finish_early(s - 1)
+            for way in (0, 1):
+                finish_late(way, s - 1)
+        if s < half - 1:
+            for way in (0, 1):
+                take_ring(way, s, 1)
+    take_ring(0, half, 0)
+    take_ring(1, half - 1, 1)
+    for way in (0, 1):
+        take_x(way, half - 1)
+    finish_early(half - 1)
+    finish_late(1, half - 1)
+    take_ring(0, half - 1, 1)
+    take_ring(1, half, 1)
+    take_x(0, half)
+    finish_late(0, half - 1)
+    finish_early(half)
+    finish_late(1, half)
+
+    low = (acc_l[:, 0:rank] + acc_r[:, rank:2 * rank]).astype(jnp.bfloat16)
+    ref_act = base[...]
+    policy = ref_act + ADAPTER_SCALE * jnp.dot(low, up_ref[...], preferred_element_type=jnp.float32)
+    t_policy = jnp.tanh(policy)
+    scores = weighted[...] * (t_policy - jnp.tanh(ref_act))
     diff = scores[0:seq, :] - scores[seq:, :]
     tile = jnp.zeros((seq, LANES), jnp.float32)
     for t in range(diff.shape[1] // LANES):
@@ -212,7 +243,7 @@
         lax.fori_loop(first, last, step, 0)
 
     each(1, n_fsdp, lambda k: ratio_copy(k).start())
-    slope = DPO_BETA * weighted * (1.0 - t_policy * t_policy)
+    slope = DPO_BETA * weighted[...] * (1.0 - t_policy * t_policy)
     grad_h = jnp.concatenate([-slope[0:seq, :], slope[seq:, :]], axis=0).astype(jnp.bfloat16)
     grad_low = ADAPTER_SCALE * lax.dot_general(
         grad_h, up_ref[...], (((1,), (1,)), ((), ())), preferred_element_type=jnp.float32
@@ -356,6 +387,7 @@
         scratch_shapes=[
             pltpu.VMEM((tokens, model), bf16),
             pltpu.VMEM((tokens, features), bf16),
+            pltpu.VMEM((tokens, features), f32),
             pltpu.VMEM((n_fsdp, rows + PACK, features), bf16),
             pltpu.VMEM((tokens, features), f32),
             pltpu.VMEM((tokens, LANES), f32),

time: 68.7 us -> 70 us (1.019)
  Pallas kernels: 67.8 us -> 68.7 us
    pallas_call x1, Pallas kernels: 66 us -> 66.9 us  [shards(): pl.pallas_call(functools.partial(kernel, n_dp, n_fsdp), out_shape=jax.Sha...]
where the time goes in v3:
time: 70 us; the launch traced here: 69.3 us
  Pallas kernels  68.7 us (98%)
    pallas_call x1, Pallas kernels, shards(): pl.pallas_call(functools.partial(kernel, n_dp, n_fsdp), out_shape=jax.Sha...  66.9 us
    pallas_call x1, Pallas kernels, shards(): pl.pallas_call(unpack, out_shape=(jax.ShapeDtypeStruct((rank, rows), f32)...  1.72 us

profile of v3, /device:TPU:0, one launch (start us, length us, event | category | flops | bytes accessed | tf_op | source)
XLA Modules:
  0.0 69.3 jit_solution(16746810849655391443)
XLA Ops:
  0.6 66.9 %dpo_adapter_gradient.1.joined = f32[80,1152]{1,0:T(8,128)} custom-call(bf16[256,8192]{1,0:T(8,128)(2,1)} %bitcast.5, bf16[256,512]{1,0:T(8,128)(2,1)} %bitcast.6, s32[2,128]{1,0:T(2,128)} %bitcast.8, bf16[1024,512]{1,0:T(8,128)(2,1)} %value_hbm.1, bf16[64,1024]{1,0:T(8,128)(2,1)} %bitcast.7, bf16[64,512]{1,0:T(8,128)(2,1)} %up_ref.1), custom_call_target="tpu_custom_call" | custom-call | tf_op jit(solution)/shard_map/dpo_adapter_gradient/pallas_call | solution.py:382
  67.6 1.7 %unpack_gradients.1 = (f32[64,1024]{1,0:T(8,128)}, f32[64,64]{1,0:T(8,128)}, f32[1]{0:T(128)}, f32[1]{0:T(128)}) custom-call(f32[80,1152]{1,0:T(8,128)} %dpo_adapter_gradient.1.joined), custom_call_target="tpu_custom_call" | custom-call | tf_op jit(solution)/shard_map/unpack_gradients/pallas_call | solution.py:428

commit v4 on v2

--- a/solution.py
+++ b/solution.py
@@ -28,7 +28,7 @@
     rank = down_ref.shape[0]
     tokens = hid.shape[0]
     seq = tokens // 2
-    swapped = weights.shape[1] * 11 // 72 // 16 * 16
+    swapped = weights.shape[1] * 13 // 72 // 16 * 16
     kept = (weights.shape[1] - 4 * swapped) // 2
     groups = rows // PACK
     up_rows = base.shape[1] // n_fsdp

time: 68.7 us -> 73.3 us (1.067)
  Pallas kernels: 67.8 us -> 72.2 us
    pallas_call x1, Pallas kernels: 66 us -> 70.5 us  [shards(): pl.pallas_call(functools.partial(kernel, n_dp, n_fsdp), out_shape=jax.Sha...]
where the time goes in v4:
time: 73.3 us; the launch traced here: 72.8 us
  Pallas kernels  72.2 us (98%)
    pallas_call x1, Pallas kernels, shards(): pl.pallas_call(functools.partial(kernel, n_dp, n_fsdp), out_shape=jax.Sha...  70.5 us
    pallas_call x1, Pallas kernels, shards(): pl.pallas_call(unpack, out_shape=(jax.ShapeDtypeStruct((rank, rows), f32)...  1.72 us

profile of v4, /device:TPU:0, one launch (start us, length us, event | category | flops | bytes accessed | tf_op | source)
XLA Modules:
  0.0 72.8 jit_solution(12213475146271313556)
XLA Ops:
  0.6 70.5 %dpo_adapter_gradient.1.joined = f32[80,1152]{1,0:T(8,128)} custom-call(bf16[256,8192]{1,0:T(8,128)(2,1)} %bitcast.5, bf16[256,512]{1,0:T(8,128)(2,1)} %bitcast.6, s32[2,128]{1,0:T(2,128)} %bitcast.8, bf16[1024,512]{1,0:T(8,128)(2,1)} %value_hbm.1, bf16[64,1024]{1,0:T(8,128)(2,1)} %bitcast.7, bf16[64,512]{1,0:T(8,128)(2,1)} %up_ref.1), custom_call_target="tpu_custom_call" | custom-call | tf_op jit(solution)/shard_map/dpo_adapter_gradient/pallas_call | solution.py:351
  71.1 1.7 %unpack_gradients.1 = (f32[64,1024]{1,0:T(8,128)}, f32[64,64]{1,0:T(8,128)}, f32[1]{0:T(128)}, f32[1]{0:T(128)}) custom-call(f32[80,1152]{1,0:T(8,128)} %dpo_adapter_gradient.1.joined), custom_call_target="tpu_custom_call" | custom-call | tf_op jit(solution)/shard_map/unpack_gradients/pallas_call | solution.py:396

commit v5 on v2

--- a/solution.py
+++ b/solution.py
@@ -18,7 +18,7 @@
     n_dp, n_fsdp,
     hid_hbm, read_hbm, resp_ref, value_hbm, down_ref, up_ref,
     out,
-    hid, read, weights, base, acc_l, acc_r, grad_low_t,
+    hid, read, weighted, weights, base, acc_l, acc_r, grad_low_t,
     ratio_buf, part, buf1, send2, buf2, total2, send3, buf3, final,
     local_sem, ring_s, ring_r, x_s, x_r, core_s, core_r,
     ratio_s, ratio_r, s1, r1, s2, r2, s3, r3, s4, r4,
@@ -93,16 +93,8 @@
 
     barrier = pltpu.get_barrier_semaphore()
 
-    def greet_fsdp(k, _):
-        pl.semaphore_signal(barrier, inc=1, device_id={"fsdp": lax.rem(me + k, n_fsdp)}, device_id_type=MESH)
-        return 0
-
-    def greet_dp(k, _):
-        pl.semaphore_signal(barrier, inc=1, device_id={"dp": lax.rem(d + k, n_dp)}, device_id_type=MESH)
-        return 0
-
-    lax.fori_loop(1, n_fsdp, greet_fsdp, 0)
-    lax.fori_loop(1, n_dp, greet_dp, 0)
+    for where in ({"fsdp": ring_peer[0]}, {"fsdp": ring_peer[1]}, {"dp": x_peer}, {"dp": core_peer}):
+        pl.semaphore_signal(barrier, inc=1, device_id=where, device_id_type=MESH)
 
     for t in range(groups // 2):
         pair = [down_ref[:, g * PACK:(g + 1) * PACK].astype(jnp.float32) for g in (2 * t, 2 * t + 1)]
@@ -113,7 +105,7 @@
         weights[me, rows:rows + PACK, used:] = jnp.zeros((PACK, weights.shape[2] - used), jnp.bfloat16)
 
     value_copy.wait()
-    pl.semaphore_wait(barrier, n_fsdp + n_dp - 2)
+    pl.semaphore_wait(barrier, 4)
 
     for kind in (0, 1):
         for way in (0, 1):
@@ -141,6 +133,13 @@
     hid_copy.wait()
     multiply(me)
 
+    read_copy.wait()
+    resp = resp_ref[...].astype(jnp.float32)
+    masks = [
+        jnp.transpose(jnp.broadcast_to(resp[i:i + 1, :], (seq, seq)))[:, 0:1] for i in (0, 1)
+    ]
+    weighted[...] = read[...].astype(jnp.float32) * jnp.concatenate(masks, axis=0)
+
     def take_ring(s, kind):
         for way in (0, 1):
             if has(way, s, kind):
@@ -186,14 +185,7 @@
     ref_act = base[...]
     policy = ref_act + ADAPTER_SCALE * jnp.dot(low, up_ref[...], preferred_element_type=jnp.float32)
     t_policy = jnp.tanh(policy)
-    read_copy.wait()
-    resp = resp_ref[...].astype(jnp.float32)
-    masks = [
-        jnp.transpose(jnp.broadcast_to(resp[i:i + 1, :], (seq, seq)))[:, 0:1] for i in (0, 1)
-    ]
-    mask = jnp.concatenate(masks, axis=0)
-    weighted = read[...].astype(jnp.float32) * mask
-    scores = weighted * (t_policy - jnp.tanh(ref_act))
+    scores = weighted[...] * (t_policy - jnp.tanh(ref_act))
     diff = scores[0:seq, :] - scores[seq:, :]
     tile = jnp.zeros((seq, LANES), jnp.float32)
     for t in range(diff.shape[1] // LANES):
@@ -212,7 +204,7 @@
         lax.fori_loop(first, last, step, 0)
 
     each(1, n_fsdp, lambda k: ratio_copy(k).start())
-    slope = DPO_BETA * weighted * (1.0 - t_policy * t_policy)
+    slope = DPO_BETA * weighted[...] * (1.0 - t_policy * t_policy)
     grad_h = jnp.concatenate([-slope[0:seq, :], slope[seq:, :]], axis=0).astype(jnp.bfloat16)
     grad_low = ADAPTER_SCALE * lax.dot_general(
         grad_h, up_ref[...], (((1,), (1,)), ((), ())), preferred_element_type=jnp.float32
@@ -267,7 +259,13 @@
         send3[k] = (total2[k] + buf2[k].astype(jnp.float32)).astype(jnp.bfloat16)
         copy3(k).start()
 
-    each(0, n_fsdp, stage1)
+    def in_order(body, count=n_fsdp):
+        def step(i):
+            odd = lax.rem(i, 2)
+            body(half + lax.div(i, 2) * (1 - odd) - lax.div(i + 1, 2) * odd)
+        each(0, count, step)
+
+    in_order(stage1)
 
     each(1, n_fsdp, lambda k: ratio_copy(k).wait())
     margin = DPO_BETA * jnp.sum(jnp.sum(ratio_buf[...], axis=0), keepdims=True)
@@ -279,11 +277,9 @@
         part[q] = part[q] * gate
         copy1(k).start()
 
-    each(1, n_fsdp, send1)
-    send1(0)
-    each(1, n_fsdp, stage2)
-    stage2(0)
-    each(1, n_fsdp, stage3)
+    in_order(send1)
+    in_order(stage2)
+    in_order(stage3, n_fsdp - 1)
     copy2(0).wait_recv()
     total2[0] = total2[0] + buf2[0].astype(jnp.float32)
 
@@ -291,8 +287,8 @@
         copy3(k).wait_recv()
         total2[0] = total2[0] + buf3[k].astype(jnp.float32)
 
-    each(1, n_fsdp, stage4)
-    final[0] = total2[0]
+    in_order(stage4, n_fsdp - 1)
+    final[0] = total2[0].astype(jnp.bfloat16)
 
     def copy4(k):
         return remote(final.at[0], final.at[k], s4.at[k], r4.at[k], dp=lax.rem(d + k, n_dp))
@@ -319,7 +315,7 @@
             total = jnp.zeros((quarter, rows + LANES), jnp.float32)
             for h in range(n_dp // 4):
                 slot = lax.rem(d - (h * 4 + x * 2 + c) + n_dp, n_dp)
-                total += final[slot]
+                total += final[slot].astype(jnp.float32)
             out[begin:begin + quarter, :] = total
     wide = rows + LANES
     out[rank:rank + 8, :] = jnp.broadcast_to(loss, (8, wide))
@@ -356,6 +352,7 @@
         scratch_shapes=[
             pltpu.VMEM((tokens, model), bf16),
             pltpu.VMEM((tokens, features), bf16),
+            pltpu.VMEM((tokens, features), f32),
             pltpu.VMEM((n_fsdp, rows + PACK, features), bf16),
             pltpu.VMEM((tokens, features), f32),
             pltpu.VMEM((tokens, LANES), f32),
@@ -369,7 +366,7 @@
             pltpu.VMEM((n_fsdp, quarter, wide), f32),
             pltpu.VMEM((n_fsdp, quarter, wide), bf16),
             pltpu.VMEM((n_fsdp, quarter, wide), bf16),
-            pltpu.VMEM((n_dp, quarter, wide), f32),
+            pltpu.VMEM((n_dp, quarter, wide), bf16),
             dma((3,)),
             dma((2, half, 2)), dma((2, half, 2)),
             dma((2, half)), dma((2, half)),

time: 68.7 us -> 67.7 us (0.985)
  Pallas kernels: 67.8 us -> 66.9 us
    pallas_call x1, Pallas kernels: 66 us -> 65.2 us  [shards(): pl.pallas_call(functools.partial(kernel, n_dp, n_fsdp), out_shape=jax.Sha...]
where the time goes in v5:
time: 67.7 us; the launch traced here: 67.5 us
  Pallas kernels  66.9 us (99%)
    pallas_call x1, Pallas kernels, shards(): pl.pallas_call(functools.partial(kernel, n_dp, n_fsdp), out_shape=jax.Sha...  65.2 us
    pallas_call x1, Pallas kernels, shards(): pl.pallas_call(unpack, out_shape=(jax.ShapeDtypeStruct((rank, rows), f32)...  1.72 us

profile of v5, /device:TPU:0, one launch (start us, length us, event | category | flops | bytes accessed | tf_op | source)
XLA Modules:
  0.0 67.5 jit_solution(13768007521544288181)
XLA Ops:
  0.6 65.2 %dpo_adapter_gradient.1.joined = f32[80,1152]{1,0:T(8,128)} custom-call(bf16[256,8192]{1,0:T(8,128)(2,1)} %bitcast.5, bf16[256,512]{1,0:T(8,128)(2,1)} %bitcast.6, s32[2,128]{1,0:T(2,128)} %bitcast.8, bf16[1024,512]{1,0:T(8,128)(2,1)} %value_hbm.1, bf16[64,1024]{1,0:T(8,128)(2,1)} %bitcast.7, bf16[64,512]{1,0:T(8,128)(2,1)} %up_ref.1), custom_call_target="tpu_custom_call" | custom-call | tf_op jit(solution)/shard_map/dpo_adapter_gradient/pallas_call | solution.py:347
  65.8 1.7 %unpack_gradients.1 = (f32[64,1024]{1,0:T(8,128)}, f32[64,64]{1,0:T(8,128)}, f32[1]{0:T(128)}, f32[1]{0:T(128)}) custom-call(f32[80,1152]{1,0:T(8,128)} %dpo_adapter_gradient.1.joined), custom_call_target="tpu_custom_call" | custom-call | tf_op jit(solution)/shard_map/unpack_gradients/pallas_call | solution.py:393

commit v6 on v5

--- a/solution.py
+++ b/solution.py
@@ -18,7 +18,7 @@
     n_dp, n_fsdp,
     hid_hbm, read_hbm, resp_ref, value_hbm, down_ref, up_ref,
     out,
-    hid, read, weighted, weights, base, acc_l, acc_r, grad_low_t,
+    hid, read, weighted, weights, base, acc, spread, grad_low_t,
     ratio_buf, part, buf1, send2, buf2, total2, send3, buf3, final,
     local_sem, ring_s, ring_r, x_s, x_r, core_s, core_r,
     ratio_s, ratio_r, s1, r1, s2, r2, s3, r3, s4, r4,
@@ -93,7 +93,12 @@
 
     barrier = pltpu.get_barrier_semaphore()
 
-    for where in ({"fsdp": ring_peer[0]}, {"fsdp": ring_peer[1]}, {"dp": x_peer}, {"dp": core_peer}):
+    greeted = [{"fsdp": ring_peer[0]}, {"fsdp": ring_peer[1]}]
+    if n_dp == 4:
+        greeted += [{"dp": x_peer}, {"dp": core_peer}]
+    else:
+        greeted += [{"dp": lax.rem(d + k, n_dp)} for k in range(1, n_dp)]
+    for where in greeted:
         pl.semaphore_signal(barrier, inc=1, device_id=where, device_id_type=MESH)
 
     for t in range(groups // 2):
@@ -105,31 +110,29 @@
         weights[me, rows:rows + PACK, used:] = jnp.zeros((PACK, weights.shape[2] - used), jnp.bfloat16)
 
     value_copy.wait()
-    pl.semaphore_wait(barrier, 4)
+    pl.semaphore_wait(barrier, len(greeted))
 
     for kind in (0, 1):
         for way in (0, 1):
             if has(way, 1, kind):
                 ring_copy(way, 1, kind, me).start()
+
+    in_left = lax.broadcasted_iota(jnp.int32, (PACK, LANES), 1) < rank
 
     def multiply(q):
         first = pl.multiple_of(q * rows, rows)
         base[...] += jnp.dot(
             hid[:, pl.ds(first, rows)], weights[q, 0:rows, :], preferred_element_type=jnp.float32
         )
-        left, right = acc_l[...], acc_r[...]
         for t in range(groups // 2):
             tile = weights[q, rows:rows + PACK, t * LANES:(t + 1) * LANES]
-            begin = pl.multiple_of(q * rows + 2 * t * PACK, PACK)
-            left += jnp.dot(hid[:, pl.ds(begin, PACK)], tile, preferred_element_type=jnp.float32)
-            begin = pl.multiple_of(q * rows + (2 * t + 1) * PACK, PACK)
-            right += jnp.dot(hid[:, pl.ds(begin, PACK)], tile, preferred_element_type=jnp.float32)
-        acc_l[...] = left
-        acc_r[...] = right
+            zero = jnp.zeros_like(tile)
+            spread[2 * t * PACK:(2 * t + 1) * PACK, :] = jnp.where(in_left, tile, zero)
+            spread[(2 * t + 1) * PACK:(2 * t + 2) * PACK, :] = jnp.where(in_left, zero, tile)
+        acc[...] += jnp.dot(hid[:, pl.ds(first, rows)], spread[...], preferred_element_type=jnp.float32)
 
     base[...] = jnp.zeros_like(base)
-    acc_l[...] = jnp.zeros_like(acc_l)
-    acc_r[...] = jnp.zeros_like(acc_r)
+    acc[...] = jnp.zeros_like(acc)
     hid_copy.wait()
     multiply(me)
 
@@ -158,30 +161,33 @@
                 x_copy(way, s, q, x_own).wait_recv()
                 core_copy(way, s, 2, q, x_own).start()
 
-    def finish(s):
-        for way in (0, 1):
-            for kind in (0, 1, 2):
-                if has(way, s, kind % 2):
-                    core_copy(way, s, kind, shard_of(way, s), core_own[kind]).wait_recv()
-        if s == half:
-            multiply(shard_of(0, s))
-        else:
-            def both(i, _):
-                multiply(at(pos + s * (2 * i - 1)))
-                return 0
-            lax.fori_loop(0, 2, both, 0)
-
-    for s in range(1, half + 1):
+    def take_core(way, s):
+        for kind in (0, 1, 2):
+            if has(way, s, kind % 2):
+                core_copy(way, s, kind, shard_of(way, s), core_own[kind]).wait_recv()
+
+    def finish(way, s):
+        take_core(way, s)
+        multiply(shard_of(way, s))
+
+    for s in range(1, half):
         take_ring(s, 0)
         if s > 1:
             take_x(s - 1)
         take_ring(s, 1)
         if s > 1:
-            finish(s - 1)
+            finish(0, s - 1)
+            finish(1, s - 1)
+    take_x(half - 1)
+    finish(1, half - 1)
+    take_ring(half, 0)
+    take_ring(half, 1)
+    finish(0, half - 1)
     take_x(half)
-    finish(half)
-
-    low = (acc_l[:, 0:rank] + acc_r[:, rank:2 * rank]).astype(jnp.bfloat16)
+    take_core(0, half)
+    finish(1, half)
+
+    low = (acc[:, 0:rank] + acc[:, rank:2 * rank]).astype(jnp.bfloat16)
     ref_act = base[...]
     policy = ref_act + ADAPTER_SCALE * jnp.dot(low, up_ref[...], preferred_element_type=jnp.float32)
     t_policy = jnp.tanh(policy)
@@ -259,13 +265,13 @@
         send3[k] = (total2[k] + buf2[k].astype(jnp.float32)).astype(jnp.bfloat16)
         copy3(k).start()
 
-    def in_order(body, count=n_fsdp):
+    def in_order(body, count=n_fsdp, begin=0):
         def step(i):
             odd = lax.rem(i, 2)
             body(half + lax.div(i, 2) * (1 - odd) - lax.div(i + 1, 2) * odd)
-        each(0, count, step)
-
-    in_order(stage1)
+        each(begin, count, step)
+
+    in_order(stage1, half)
 
     each(1, n_fsdp, lambda k: ratio_copy(k).wait())
     margin = DPO_BETA * jnp.sum(jnp.sum(ratio_buf[...], axis=0), keepdims=True)
@@ -277,7 +283,12 @@
         part[q] = part[q] * gate
         copy1(k).start()
 
-    in_order(send1)
+    def both1(k):
+        stage1(k)
+        send1(k)
+
+    in_order(send1, half)
+    in_order(both1, n_fsdp, half)
     in_order(stage2)
     in_order(stage3, n_fsdp - 1)
     copy2(0).wait_recv()
@@ -356,7 +367,7 @@
             pltpu.VMEM((n_fsdp, rows + PACK, features), bf16),
             pltpu.VMEM((tokens, features), f32),
             pltpu.VMEM((tokens, LANES), f32),
-            pltpu.VMEM((tokens, LANES), f32),
+            pltpu.VMEM((rows, LANES), bf16),
             pltpu.VMEM((rank, tokens), bf16),
             pltpu.VMEM((n_fsdp, 8, LANES), f32),
             pltpu.VMEM((n_fsdp, rank, wide), f32),

time: 67.7 us -> 69.8 us (1.031)
  Pallas kernels: 66.9 us -> 69 us
    pallas_call x1, Pallas kernels: 65.2 us -> 67.3 us  [shards(): pl.pallas_call(functools.partial(kernel, n_dp, n_fsdp), out_shape=jax.Sha...]
where the time goes in v6:
time: 69.8 us; the launch traced here: 69.6 us
  Pallas kernels  69 us (99%)
    pallas_call x1, Pallas kernels, shards(): pl.pallas_call(functools.partial(kernel, n_dp, n_fsdp), out_shape=jax.Sha...  67.3 us
    pallas_call x1, Pallas kernels, shards(): pl.pallas_call(unpack, out_shape=(jax.ShapeDtypeStruct((rank, rows), f32)...  1.72 us

profile of v6, /device:TPU:0, one launch (start us, length us, event | category | flops | bytes accessed | tf_op | source)
XLA Modules:
  0.0 69.6 jit_solution(8141541341566035294)
XLA Ops:
  0.6 67.3 %dpo_adapter_gradient.1.joined = f32[80,1152]{1,0:T(8,128)} custom-call(bf16[256,8192]{1,0:T(8,128)(2,1)} %bitcast.5, bf16[256,512]{1,0:T(8,128)(2,1)} %bitcast.6, s32[2,128]{1,0:T(2,128)} %bitcast.8, bf16[1024,512]{1,0:T(8,128)(2,1)} %value_hbm.1, bf16[64,1024]{1,0:T(8,128)(2,1)} %bitcast.7, bf16[64,512]{1,0:T(8,128)(2,1)} %up_ref.1), custom_call_target="tpu_custom_call" | custom-call | tf_op jit(solution)/shard_map/dpo_adapter_gradient/pallas_call | solution.py:358
  67.9 1.7 %unpack_gradients.1 = (f32[64,1024]{1,0:T(8,128)}, f32[64,64]{1,0:T(8,128)}, f32[1]{0:T(128)}, f32[1]{0:T(128)}) custom-call(f32[80,1152]{1,0:T(8,128)} %dpo_adapter_gradient.1.joined), custom_call_target="tpu_custom_call" | custom-call | tf_op jit(solution)/shard_map/unpack_gradients/pallas_call | solution.py:404

commit v7 on v6

--- a/solution.py
+++ b/solution.py
@@ -28,7 +28,7 @@
     rank = down_ref.shape[0]
     tokens = hid.shape[0]
     seq = tokens // 2
-    swapped = weights.shape[1] * 11 // 72 // 16 * 16
+    swapped = weights.shape[1] * 10 // 72 // 16 * 16
     kept = (weights.shape[1] - 4 * swapped) // 2
     groups = rows // PACK
     up_rows = base.shape[1] // n_fsdp
@@ -170,7 +170,7 @@
         take_core(way, s)
         multiply(shard_of(way, s))
 
-    for s in range(1, half):
+    for s in range(1, half + 1):
         take_ring(s, 0)
         if s > 1:
             take_x(s - 1)
@@ -178,11 +178,6 @@
         if s > 1:
             finish(0, s - 1)
             finish(1, s - 1)
-    take_x(half - 1)
-    finish(1, half - 1)
-    take_ring(half, 0)
-    take_ring(half, 1)
-    finish(0, half - 1)
     take_x(half)
     take_core(0, half)
     finish(1, half)

time: 69.8 us -> 68.1 us (0.976)
  Pallas kernels: 69 us -> 67.3 us
    pallas_call x1, Pallas kernels: 67.3 us -> 65.6 us  [shards(): pl.pallas_call(functools.partial(kernel, n_dp, n_fsdp), out_shape=jax.Sha...]
where the time goes in v7:
time: 68.1 us; the launch traced here: 68 us
  Pallas kernels  67.3 us (99%)
    pallas_call x1, Pallas kernels, shards(): pl.pallas_call(functools.partial(kernel, n_dp, n_fsdp), out_shape=jax.Sha...  65.6 us
    pallas_call x1, Pallas kernels, shards(): pl.pallas_call(unpack, out_shape=(jax.ShapeDtypeStruct((rank, rows), f32)...  1.72 us

profile of v7, /device:TPU:0, one launch (start us, length us, event | category | flops | bytes accessed | tf_op | source)
XLA Modules:
  0.0 68.0 jit_solution(14485286728396434116)
XLA Ops:
  0.6 65.6 %dpo_adapter_gradient.1.joined = f32[80,1152]{1,0:T(8,128)} custom-call(bf16[256,8192]{1,0:T(8,128)(2,1)} %bitcast.5, bf16[256,512]{1,0:T(8,128)(2,1)} %bitcast.6, s32[2,128]{1,0:T(2,128)} %bitcast.8, bf16[1024,512]{1,0:T(8,128)(2,1)} %value_hbm.1, bf16[64,1024]{1,0:T(8,128)(2,1)} %bitcast.7, bf16[64,512]{1,0:T(8,128)(2,1)} %up_ref.1), custom_call_target="tpu_custom_call" | custom-call | tf_op jit(solution)/shard_map/dpo_adapter_gradient/pallas_call | solution.py:353
  66.2 1.7 %unpack_gradients.1 = (f32[64,1024]{1,0:T(8,128)}, f32[64,64]{1,0:T(8,128)}, f32[1]{0:T(128)}, f32[1]{0:T(128)}) custom-call(f32[80,1152]{1,0:T(8,128)} %dpo_adapter_gradient.1.joined), custom_call_target="tpu_custom_call" | custom-call | tf_op jit(solution)/shard_map/unpack_gradients/pallas_call | solution.py:399

commit v8 on v7

--- a/solution.py
+++ b/solution.py
@@ -28,7 +28,7 @@
     rank = down_ref.shape[0]
     tokens = hid.shape[0]
     seq = tokens // 2
-    swapped = weights.shape[1] * 10 // 72 // 16 * 16
+    swapped = weights.shape[1] * 11 // 72 // 16 * 16
     kept = (weights.shape[1] - 4 * swapped) // 2
     groups = rows // PACK
     up_rows = base.shape[1] // n_fsdp

time: 68.1 us -> 67.8 us (level)
  no operation moved by 1% of the time
where the time goes in v8:
time: 67.8 us; the launch traced here: 67.6 us
  Pallas kernels  67 us (99%)
    pallas_call x1, Pallas kernels, shards(): pl.pallas_call(functools.partial(kernel, n_dp, n_fsdp), out_shape=jax.Sha...  65.3 us
    pallas_call x1, Pallas kernels, shards(): pl.pallas_call(unpack, out_shape=(jax.ShapeDtypeStruct((rank, rows), f32)...  1.72 us

profile of v8, /device:TPU:0, one launch (start us, length us, event | category | flops | bytes accessed | tf_op | source)
XLA Modules:
  0.0 67.6 jit_solution(3942765223527875113)
XLA Ops:
  0.6 65.3 %dpo_adapter_gradient.1.joined = f32[80,1152]{1,0:T(8,128)} custom-call(bf16[256,8192]{1,0:T(8,128)(2,1)} %bitcast.5, bf16[256,512]{1,0:T(8,128)(2,1)} %bitcast.6, s32[2,128]{1,0:T(2,128)} %bitcast.8, bf16[1024,512]{1,0:T(8,128)(2,1)} %value_hbm.1, bf16[64,1024]{1,0:T(8,128)(2,1)} %bitcast.7, bf16[64,512]{1,0:T(8,128)(2,1)} %up_ref.1), custom_call_target="tpu_custom_call" | custom-call | tf_op jit(solution)/shard_map/dpo_adapter_gradient/pallas_call | solution.py:353
  65.9 1.7 %unpack_gradients.1 = (f32[64,1024]{1,0:T(8,128)}, f32[64,64]{1,0:T(8,128)}, f32[1]{0:T(128)}, f32[1]{0:T(128)}) custom-call(f32[80,1152]{1,0:T(8,128)} %dpo_adapter_gradient.1.joined), custom_call_target="tpu_custom_call" | custom-call | tf_op jit(solution)/shard_map/unpack_gradients/pallas_call | solution.py:399

commit v9 on v8

--- a/solution.py
+++ b/solution.py
@@ -21,6 +21,7 @@
     hid, read, weighted, weights, base, acc, spread, grad_low_t,
     ratio_buf, part, buf1, send2, buf2, total2, send3, buf3, final,
     local_sem, ring_s, ring_r, x_s, x_r, core_s, core_r,
+    first_s, first_r, first_xs, first_xr,
     ratio_s, ratio_r, s1, r1, s2, r2, s3, r3, s4, r4,
 ):
     half = n_fsdp // 2
@@ -81,6 +82,20 @@
         ref = piece(q, kind, p)
         return remote(ref, ref, core_s.at[way, s - 1, kind], core_r.at[way, s - 1, kind], dp=core_peer)
 
+    cut = (swapped // 2 + 15) // 16 * 16
+
+    def part_of(q, p, h):
+        begin = pl.multiple_of(p * swapped + h * cut, 16)
+        return weights.at[q, pl.ds(begin, swapped - cut if h else cut), :]
+
+    def first_ring(way, h, q):
+        ref = part_of(q, own[0], h)
+        return remote(ref, ref, first_s.at[way, h], first_r.at[way, h], fsdp=ring_peer[way])
+
+    def first_x(way, h, q, p):
+        ref = part_of(q, p, h)
+        return remote(ref, ref, first_xs.at[way, h], first_xr.at[way, h], dp=x_peer)
+
     def has(way, s, kind):
         return s < half or (s == half and way == kind)
 
@@ -112,10 +127,11 @@
     value_copy.wait()
     pl.semaphore_wait(barrier, len(greeted))
 
-    for kind in (0, 1):
+    for h in (0, 1):
         for way in (0, 1):
-            if has(way, 1, kind):
-                ring_copy(way, 1, kind, me).start()
+            first_ring(way, h, me).start()
+    for way in (0, 1):
+        ring_copy(way, 1, 1, me).start()
 
     in_left = lax.broadcasted_iota(jnp.int32, (PACK, LANES), 1) < rank
 
@@ -143,7 +159,22 @@
     ]
     weighted[...] = read[...].astype(jnp.float32) * jnp.concatenate(masks, axis=0)
 
+    def take_first():
+        for h in (0, 1):
+            for way in (0, 1):
+                q = shard_of(way, 1)
+                first_ring(way, h, q).wait_recv()
+                first_x(way, h, q, own[0]).start()
+        for way in (0, 1):
+            q = shard_of(way, 1)
+            if has(way, 2, 0):
+                ring_copy(way, 2, 0, q).start()
+            core_copy(way, 1, 0, q, own[0]).start()
+
     def take_ring(s, kind):
+        if s == 1 and kind == 0:
+            take_first()
+            return
         for way in (0, 1):
             if has(way, s, kind):
                 q = shard_of(way, s)
@@ -158,7 +189,11 @@
         for way in (0, 1):
             if has(way, s, 0):
                 q = shard_of(way, s)
-                x_copy(way, s, q, x_own).wait_recv()
+                if s == 1:
+                    first_x(way, 0, q, x_own).wait_recv()
+                    first_x(way, 1, q, x_own).wait_recv()
+                else:
+                    x_copy(way, s, q, x_own).wait_recv()
                 core_copy(way, s, 2, q, x_own).start()
 
     def take_core(way, s):
@@ -305,10 +340,16 @@
         for way in (0, 1):
             for kind in (0, 1):
                 if has(way, s, kind):
-                    ring_copy(way, s, kind, me).wait_send()
+                    if s == 1 and kind == 0:
+                        for h in (0, 1):
+                            first_ring(way, h, me).wait_send()
+                            first_x(way, h, me, own[0]).wait_send()
+                    else:
+                        ring_copy(way, s, kind, me).wait_send()
                     core_copy(way, s, kind, me, own[kind]).wait_send()
             if has(way, s, 0):
-                x_copy(way, s, me, own[0]).wait_send()
+                if s > 1:
+                    x_copy(way, s, me, own[0]).wait_send()
                 core_copy(way, s, 2, me, x_own).wait_send()
     each(0, n_fsdp, lambda k: copy1(k).wait_send())
     each(0, n_fsdp, lambda k: copy2(k).wait_send())
@@ -377,6 +418,7 @@
             dma((2, half, 2)), dma((2, half, 2)),
             dma((2, half)), dma((2, half)),
             dma((2, half, 3)), dma((2, half, 3)),
+            dma((2, 2)), dma((2, 2)), dma((2, 2)), dma((2, 2)),
             dma((n_fsdp,)), dma((n_fsdp,)),
             dma((n_fsdp,)), dma((n_fsdp,)),
             dma((n_fsdp,)), dma((n_fsdp,)),

time: 67.8 us -> 68 us (level)
  no operation moved by 1% of the time
where the time goes in v9:
time: 68 us; the launch traced here: 67.8 us
  Pallas kernels  67.1 us (99%)
    pallas_call x1, Pallas kernels, shards(): pl.pallas_call(functools.partial(kernel, n_dp, n_fsdp), out_shape=jax.Sha...  65.4 us
    pallas_call x1, Pallas kernels, shards(): pl.pallas_call(unpack, out_shape=(jax.ShapeDtypeStruct((rank, rows), f32)...  1.72 us

profile of v9, /device:TPU:0, one launch (start us, length us, event | category | flops | bytes accessed | tf_op | source)
XLA Modules:
  0.0 67.8 jit_solution(13745704730923817804)
XLA Ops:
  0.6 65.4 %dpo_adapter_gradient.1.joined = f32[80,1152]{1,0:T(8,128)} custom-call(bf16[256,8192]{1,0:T(8,128)(2,1)} %bitcast.5, bf16[256,512]{1,0:T(8,128)(2,1)} %bitcast.6, s32[2,128]{1,0:T(2,128)} %bitcast.8, bf16[1024,512]{1,0:T(8,128)(2,1)} %value_hbm.1, bf16[64,1024]{1,0:T(8,128)(2,1)} %bitcast.7, bf16[64,512]{1,0:T(8,128)(2,1)} %up_ref.1), custom_call_target="tpu_custom_call" | custom-call | tf_op jit(solution)/shard_map/dpo_adapter_gradient/pallas_call | solution.py:394
  66.1 1.7 %unpack_gradients.1 = (f32[64,1024]{1,0:T(8,128)}, f32[64,64]{1,0:T(8,128)}, f32[1]{0:T(128)}, f32[1]{0:T(128)}) custom-call(f32[80,1152]{1,0:T(8,128)} %dpo_adapter_gradient.1.joined), custom_call_target="tpu_custom_call" | custom-call | tf_op jit(solution)/shard_map/unpack_gradients/pallas_call | solution.py:441
